TPU v7x, 32 devices: a whole 2x2x4 slice. The times are simulated.
32 devices in a mesh: tracer: 4 (over y, x), tile: 8 (over z, core).
Axes of the slice: x: 2, y: 2, z: 4, core: 2. Of those that a mesh axis runs over, the one named last changes fastest.
Arguments:
- tracers: float32 [192, 8, 128, 128], P('tracer', None, 'tile'), may hold values from 0.1 to 2
- air_mass: float32 [4, 8, 128, 128], P('tracer', None, 'tile'), may hold values from 1 to 2
- flux_x: float32 [4, 8, 128, 128], P('tracer', None, 'tile'), may hold values from -0.2 to 0.2
- flux_y: float32 [4, 8, 128, 128], P('tracer', None, 'tile'), may hold values from -0.2 to 0.2
- flux_z: float32 [4, 8, 128, 128], P('tracer', None, 'tile'), may hold values from -0.05 to 0.05
- reactants: int32 [512, 2], replicated, may hold values from 0 to 191
- products: int32 [512, 192], replicated, may hold values 0 or 1
- rate_coeff: float32 [512], replicated, may hold values from 0.01 to 0.1
- record_of_step: int32 [2], replicated, may hold values from 0 to 3
Outputs:
- tracers_out: float32 [192, 8, 128, 128], P('tracer', None, 'tile')
Inputs may be any that keep to these rules, and one draw needn't show every extreme that they name: A reaction's two reactants may be the same tracer.
All inputs are finite; a program needn't handle non-finite values.
Results may differ from a plain program's by a relative error of at most 0.0014.
Values may be sent and summed in bfloat16 or wider, within the bound.
A program may use at most 128 MiB of HBM per device.

v0:
```python
import functools

import jax
import jax.numpy as jnp
from jax import lax
from jax.experimental import pallas as pl
from jax.experimental.pallas import tpu as pltpu
from jax.sharding import PartitionSpec as P

STEPS = 2
PIECES = 4
WIDE = 4


def face_weights(flux, mass_low, mass_high):
    courant = jnp.abs(flux) / jnp.maximum(jnp.where(flux > 0, mass_low, mass_high), 0.5)
    square = courant * courant
    return (
        flux * (1.0 - 2.0 * courant + square),
        flux * (square - courant),
        flux * (3.0 * courant - 2.0 * square),
    )


def edge_value(outer_low, low, high, outer_high):
    value = (7.0 / 12.0) * (low + high) - (1.0 / 12.0) * (outer_low + outer_high)
    return jnp.minimum(jnp.maximum(value, jnp.minimum(low, high)), jnp.maximum(low, high))


def face_value(flux, weights, edge, edge_low, edge_high, low, high):
    up = flux > 0
    return (
        weights[0] * edge
        + weights[1] * jnp.where(up, edge_low, edge_high)
        + weights[2] * jnp.where(up, low, high)
    )


def rolled_difference(q, flux, weights, axis, place):
    size = q.shape[axis]
    low = jnp.where(place >= 1, pltpu.roll(q, 1, axis), 0.0)
    outer_low = jnp.where(place >= 2, pltpu.roll(q, 2, axis), 0.0)
    outer_high = jnp.where(place < size - 1, pltpu.roll(q, size - 1, axis), 0.0)
    edge = edge_value(outer_low, low, q, outer_high)
    last = (7.0 / 12.0) * q - (1.0 / 12.0) * low
    last = jnp.minimum(jnp.maximum(last, jnp.minimum(q, 0.0)), jnp.maximum(q, 0.0))
    edge_high = jnp.where(place == size - 1, last, pltpu.roll(edge, size - 1, axis))
    faces = face_value(flux, weights, edge, pltpu.roll(edge, 1, axis), edge_high, low, q)
    return pltpu.roll(faces, size - 1, axis) - faces


def step_kernel(
    n, chunks, q_ref, low_ref, high_ref, air_ref, fx_ref, fy_ref, fz_ref, pick_ref, net_ref, rate_ref,
    out_ref, wx, wy, wz, inverse, lines, send_one, recv_one, send_two, recv_two, back,
    send_sem, recv_sem, send_sem2, recv_sem2,
):
    tracers, rows, levels, columns = q_ref.shape
    padded = back.shape[0] // (rows * levels)
    width = padded // chunks
    in_chunk = tracers // chunks
    held = rows * levels // n
    reactions = rate_ref.shape[0]
    me = lax.axis_index("tracer")
    peers = [lax.rem(me + k, n) for k in range(n)]

    barrier = pltpu.get_barrier_semaphore()
    for peer in peers[1:]:
        pl.semaphore_signal(
            barrier, inc=1, device_id={"tracer": peer}, device_id_type=pl.DeviceIdType.MESH
        )
    pl.semaphore_wait(barrier, n - 1)

    shape = (levels, columns)
    level = lax.broadcasted_iota(jnp.int32, shape, 0)
    column = lax.broadcasted_iota(jnp.int32, shape, 1)

    @pl.loop(0, rows + 1)
    def _(r):
        for i, w in enumerate(face_weights(fx_ref[r], air_ref[r], air_ref[r + 1])):
            wx[i, r] = w

    @pl.loop(0, rows)
    def _(r):
        mass = air_ref[r + 1]
        south, bottom = fy_ref[r], fz_ref[r]
        for i, w in enumerate(face_weights(south, pltpu.roll(mass, 1, 1), mass)):
            wy[i, r] = w
        for i, w in enumerate(face_weights(bottom, pltpu.roll(mass, 1, 0), mass)):
            wz[i, r] = w
        new_mass = (
            mass
            - (fx_ref[r + 1] - fx_ref[r])
            - (pltpu.roll(south, columns - 1, 1) - south)
            - (pltpu.roll(bottom, levels - 1, 0) - bottom)
        )
        inverse[r] = 1.0 / new_mass

    if in_chunk != width:
        lines[...] = jnp.zeros_like(lines)

    def copy_one(k, c):
        return pltpu.make_async_remote_copy(
            src_ref=send_one.at[peers[k], c],
            dst_ref=recv_one.at[me, c],
            send_sem=send_sem.at[k - 1, c],
            recv_sem=recv_sem.at[k - 1, c],
            device_id={"tracer": peers[k]},
            device_id_type=pl.DeviceIdType.MESH,
        )

    def arrived_one(k, c):
        source = peers[n - k]
        return pltpu.make_async_remote_copy(
            src_ref=send_one.at[source, c],
            dst_ref=recv_one.at[source, c],
            send_sem=send_sem.at[k - 1, c],
            recv_sem=recv_sem.at[k - 1, c],
            device_id={"tracer": source},
            device_id_type=pl.DeviceIdType.MESH,
        )

    for c in range(chunks):

        @pl.loop(0, in_chunk)
        def _(s):
            t = c * in_chunk + s

            def cell(r):
                if r < 0:
                    return low_ref[t, r + 3]
                return q_ref[t, r] if r < rows else high_ref[t, r - rows]

            q = {r: cell(r) for r in range(-3, 2)}
            edges = {r: edge_value(q[r - 2], q[r - 1], q[r], q[r + 1]) for r in (-1, 0)}
            before = None
            for r in range(rows + 1):
                q[r + 2] = cell(r + 2)
                edges[r + 1] = edge_value(q[r - 1], q[r], q[r + 1], q[r + 2])
                face = face_value(
                    fx_ref[r], [wx[i, r] for i in range(3)],
                    edges[r], edges[r - 1], edges[r + 1], q[r - 1], q[r],
                )
                if r > 0:
                    p = r - 1
                    total = face - before
                    total += rolled_difference(q[p], fy_ref[p], [wy[i, p] for i in range(3)], 1, column)
                    total += rolled_difference(q[p], fz_ref[p], [wz[i, p] for i in range(3)], 0, level)
                    advected = (air_ref[p + 1] * q[p] - total) * inverse[p]
                    out_ref[t, p] = advected
                    lines[pl.ds(p * levels * width + s, levels, stride=width), :] = advected
                before = face

        for d in range(n):
            size = held * width
            send_one[d, c] = (
                lines[d * size : (d + 1) * size, :].astype(jnp.bfloat16).reshape(held, width, columns)
            )
        for k in range(1, n):
            copy_one(k, c).start()
        recv_one[me, c] = send_one[me, c]

    for c in range(chunks):
        for k in range(1, n):
            arrived_one(k, c).wait_recv()

    part = held // PIECES

    def copy_two(k, h):
        span = pl.ds(h * part, part)
        return pltpu.make_async_remote_copy(
            src_ref=send_two.at[peers[k], span],
            dst_ref=recv_two.at[me, span],
            send_sem=send_sem2.at[k - 1, h],
            recv_sem=recv_sem2.at[k - 1, h],
            device_id={"tracer": peers[k]},
            device_id_type=pl.DeviceIdType.MESH,
        )

    def arrived_two(k, h):
        span = pl.ds(h * part, part)
        source = peers[n - k]
        return pltpu.make_async_remote_copy(
            src_ref=send_two.at[source, span],
            dst_ref=recv_two.at[source, span],
            send_sem=send_sem2.at[k - 1, h],
            recv_sem=recv_sem2.at[k - 1, h],
            device_id={"tracer": source},
            device_id_type=pl.DeviceIdType.MESH,
        )

    wide = min(WIDE, part)
    for h in range(PIECES):

        @pl.loop(0, part // wide)
        def _(g):
            first = h * part + g * wide
            conc = jnp.concatenate(
                [
                    jnp.concatenate(
                        [recv_one[d, c, first + i] for d in range(n) for c in range(chunks)], 0
                    )
                    for i in range(wide)
                ],
                1,
            )
            one = jnp.dot(pick_ref[:reactions], conc, preferred_element_type=jnp.float32)
            two = jnp.dot(pick_ref[reactions:], conc, preferred_element_type=jnp.float32)
            rate = (rate_ref[...] * one * two).astype(jnp.bfloat16)
            change = jnp.dot(net_ref[...], rate, preferred_element_type=jnp.float32).astype(jnp.bfloat16)
            for d in range(n):
                for i in range(wide):
                    send_two[d, first + i] = change[
                        d * padded : (d + 1) * padded, i * columns : (i + 1) * columns
                    ]

        for k in range(1, n):
            copy_two(k, h).start()
        span = pl.ds(h * part, part)
        recv_two[me, span] = send_two[me, span]

    for h in range(PIECES):
        for k in range(1, n):
            arrived_two(k, h).wait_recv()

    size = held * padded
    for d in range(n):
        back[d * size : (d + 1) * size, :] = (
            recv_two[d].astype(jnp.float32).reshape(size, columns)
        )

    @pl.loop(0, tracers)
    def _(t):
        for r in range(rows):
            out_ref[t, r] += back[pl.ds(r * levels * padded + t, levels, stride=padded), :]

    for k in range(1, n):
        for c in range(chunks):
            copy_one(k, c).wait_send()
        for h in range(PIECES):
            copy_two(k, h).wait_send()


def step(n, q, low, high, air, fx, fy, fz, pick, net, rate):
    tracers, rows, levels, columns = q.shape
    padded = net.shape[0] // n
    chunks = tracers // 16 if tracers % 16 == 0 else 1
    width = padded // chunks
    held = rows * levels // n
    vmem = pl.BlockSpec(memory_space=pltpu.VMEM)
    f32, bf16 = jnp.float32, jnp.bfloat16
    return pl.pallas_call(
        functools.partial(step_kernel, n, chunks),
        out_shape=jax.ShapeDtypeStruct(q.shape, f32),
        in_specs=[vmem] * 10,
        out_specs=vmem,
        scratch_shapes=[
            pltpu.VMEM((3, rows + 1, levels, columns), f32),
            pltpu.VMEM((3, rows, levels, columns), f32),
            pltpu.VMEM((3, rows, levels, columns), f32),
            pltpu.VMEM((rows, levels, columns), f32),
            pltpu.VMEM((rows * levels * width, columns), f32),
            pltpu.VMEM((n, chunks, held, width, columns), bf16),
            pltpu.VMEM((n, chunks, held, width, columns), bf16),
            pltpu.VMEM((n, held, padded, columns), bf16),
            pltpu.VMEM((n, held, padded, columns), bf16),
            pltpu.VMEM((rows * levels * padded, columns), f32),
            pltpu.SemaphoreType.DMA((n - 1, chunks)),
            pltpu.SemaphoreType.DMA((n - 1, chunks)),
            pltpu.SemaphoreType.DMA((n - 1, PIECES)),
            pltpu.SemaphoreType.DMA((n - 1, PIECES)),
        ],
        compiler_params=pltpu.CompilerParams(
            collective_id=0, has_side_effects=True, vmem_limit_bytes=50 * 1024 * 1024
        ),
    )(q, low, high, air, fx, fy, fz, pick, net, rate)


def halos(block, dim):
    count = lax.axis_size("tile")
    forward = [(i, i + 1) for i in range(count - 1)]
    backward = [(target, source) for source, target in forward]
    size = block.shape[dim]
    low = lax.ppermute(lax.slice_in_dim(block, size - 3, size, axis=dim), "tile", forward)
    high = lax.ppermute(lax.slice_in_dim(block, 0, 3, axis=dim), "tile", backward)
    return low, high


def pad_blocks(matrix, n, padded):
    own = matrix.shape[1] // n
    blocks = matrix.reshape(matrix.shape[0], n, own)
    return jnp.pad(blocks, ((0, 0), (0, 0), (0, padded - own))).reshape(matrix.shape[0], n * padded)


def per_device(
    tracers, air_mass, flux_x, flux_y, flux_z, reactants, products, rate_coeff, record_of_step
):
    n = lax.axis_size("tracer")
    reactions, species = products.shape
    padded = -(-tracers.shape[0] // 16) * 16
    ident = lax.broadcasted_iota(jnp.int32, (reactions, species), 1)
    first_hot = (reactants[:, 0:1] == ident).astype(jnp.float32)
    second_hot = (reactants[:, 1:2] == ident).astype(jnp.float32)
    pick = pad_blocks(jnp.concatenate([first_hot, second_hot], 0), n, padded).astype(jnp.bfloat16)
    net = pad_blocks(products.astype(jnp.float32) - first_hot - second_hot, n, padded)
    net = net.T.astype(jnp.bfloat16)
    rate = rate_coeff[:, None]
    mixing = jnp.swapaxes(tracers, 1, 2)
    rows = mixing.shape[1]
    fields = jnp.swapaxes(jnp.concatenate([air_mass, flux_x, flux_y, flux_z], 0), 1, 2)
    mine = lax.axis_index("tracer")
    chosen = jnp.stack([jnp.where(record_of_step[s] == mine, fields, 0.0) for s in range(STEPS)])
    weather = lax.psum(chosen, "tracer")
    below, above = halos(weather[:, :2], 2)
    place = lax.axis_index("tile") * rows + lax.broadcasted_iota(jnp.int32, weather.shape[2:], 0)
    level = lax.broadcasted_iota(jnp.int32, weather.shape[2:], 1)
    column = lax.broadcasted_iota(jnp.int32, weather.shape[2:], 2)
    for s in range(STEPS):
        air, east, south, bottom = (weather[s, i] for i in range(4))
        air = jnp.concatenate([below[s, 0, 2:3], air, above[s, 0, :1]], 0)
        east = jnp.concatenate([jnp.where(place == 0, 0.0, east), above[s, 1, :1]], 0)
        south = jnp.where(column == 0, 0.0, south)
        bottom = jnp.where(level == 0, 0.0, bottom)
        low, high = halos(mixing, 1)
        mixing = step(n, mixing, low, high, air, east, south, bottom, pick, net, rate)
    return jnp.swapaxes(mixing, 1, 2)


def solution(mesh):
    split = P("tracer", None, "tile", None)
    return jax.shard_map(
        per_device, mesh=mesh, in_specs=(split,) * 5 + (P(),) * 4, out_specs=split, check_vma=False
    )
```

profile of v0, /device:TPU:8, one launch (start us, length us, event | category | flops | bytes accessed | tf_op | source)
XLA Modules:
  0.0 200.7 jit_solution(16636949671044030890)
XLA Ops:
  6.5 1.3 fusion.12
  9.1 0.9 copy_dynamic-update-slice_fusion.3
  9.9 0.9 copy_dynamic-update-slice_fusion.2
  10.8 0.9 copy_dynamic-update-slice_fusion.1
  11.7 0.9 copy_dynamic-update-slice_fusion
  12.6 0.8 pad_maximum_fusion
  13.4 0.0 all-reduce.2.cloned.1.call-update
  13.4 0.0 copy-start.1
  13.4 0.0 copy-start.2
  13.5 3.3 %copy.33 = f32[48,8,16,128]{3,1,2,0:T(8,128)S(1)} copy(f32[48,8,16,128]{3,2,1,0:T(8,128)} %param.9) | data formatting | bytes 6291456 | tf_op args[0]
  16.8 0.0 copy-start
  16.8 0.1 fusion.9
  16.9 1.9 collective-permute-start.1
  18.8 2.4 %collective-permute-start = (f32[48,3,8,128]{3,2,1,0:T(8,128)S(1)}, f32[48,3,8,128]{3,2,1,0:T(8,128)S(1)}, u32[]{:S(2)}, u32[]{:S(2)}) collective-permute-start(f32[48,3,8,128]{3,2,1,0:T(8,128)S(1)} %get-tuple-element.8), channel_id=1, source_target_pairs={{0,1},{1,2},{2,3},{3,4},{4,5},{5,6},{6,7},{8,9},{9,10},{10,11},{11... | collective-permute-start | bytes 1769480 | tf_op jit(solution)/shard_map/ppermute | solution.py:283
  21.3 0.1 copy.24.rate_ref
  21.4 0.1 convert_convert_fusion
  21.6 0.2 copy.23.pick_ref
  21.8 1.1 fusion.1.net_ref
  22.9 37.2 %all-reduce.2.cloned.1.call-done = f32[2,4,16,8,128]{4,3,2,1,0:T(8,128)} async-done(((f32[2,4,16,8,128]{4,3,2,1,0:T(8,128)}), f32[2,4,16,8,128]{4,3,2,1,0:T(8,128)}) %all-reduce.2.cloned.1.call-update) | async-done | bytes 524304 | tf_op jit(solution)/shard_map/psum | solution.py:312
  60.1 0.8 fusion.10
  60.9 1.9 collective-permute-start.2
  62.8 3.6 %collective-permute-start.3 = (f32[2,2,3,8,128]{4,3,2,1,0:T(8,128)S(1)}, f32[2,2,3,8,128]{4,3,2,1,0:T(8,128)S(1)}, u32[]{:S(2)}, u32[]{:S(2)}) collective-permute-start(f32[2,2,3,8,128]{4,3,2,1,0:T(8,128)S(1)} %get-tuple-element.22), channel_id=1, source_target_pairs={{1,0},{2,1},{3,2},{4,3},{5,4},{6,5},{7,6},{9,8},{10,9},{11,10},{12... | collective-permute-start | bytes 147464 | tf_op jit(solution)/shard_map/ppermute | solution.py:284
  66.5 1.1 fusion.2
  67.6 0.9 slice_bitcast_fusion.3
  68.6 54.7 %shard_map.91.q_ref = f32[48,16,8,128]{3,2,1,0:T(8,128)} custom-call(f32[48,16,8,128]{3,2,1,0:T(8,128)} %bitcast.60, f32[48,3,8,128]{3,2,1,0:T(8,128)S(1)} %collective-permute-done.low_ref, f32[48,3,8,128]{3,2,1,0:T(8,128)S(1)} %collective-permute-done.1.high_ref, f32[18,8,128]{2,1,0:T(8,128)S(1)} %pad_maximum_fusion.2.air_ref, ...), custom_call_target="tpu_custom_call" | custom-call | tf_op jit(solution)/shard_map/pallas_call | solution.py:251
  123.3 1.3 fusion.8
  124.6 1.9 collective-permute-start.5
  126.5 2.4 %collective-permute-start.4 = (f32[48,3,8,128]{3,2,1,0:T(8,128)S(1)}, f32[48,3,8,128]{3,2,1,0:T(8,128)S(1)}, u32[]{:S(2)}, u32[]{:S(2)}) collective-permute-start(f32[48,3,8,128]{3,2,1,0:T(8,128)S(1)} %get-tuple-element.6), channel_id=1, source_target_pairs={{0,1},{1,2},{2,3},{3,4},{4,5},{5,6},{6,7},{8,9},{9,10},{10,11},{11... | collective-permute-start | bytes 1769480 | tf_op jit(solution)/shard_map/ppermute | solution.py:283
  129.0 4.9 %collective-permute-done.5.high_ref = f32[48,3,8,128]{3,2,1,0:T(8,128)S(1)} collective-permute-done((f32[48,3,8,128]{3,2,1,0:T(8,128)S(1)}, f32[48,3,8,128]{3,2,1,0:T(8,128)S(1)}, u32[]{:S(2)}, u32[]{:S(2)}) %collective-permute-start.5) | collective-permute-done | bytes 589856 | tf_op jit(solution)/shard_map/ppermute | solution.py:284
  133.9 3.8 %collective-permute-done.4.low_ref = f32[48,3,8,128]{3,2,1,0:T(8,128)S(1)} collective-permute-done((f32[48,3,8,128]{3,2,1,0:T(8,128)S(1)}, f32[48,3,8,128]{3,2,1,0:T(8,128)S(1)}, u32[]{:S(2)}, u32[]{:S(2)}) %collective-permute-start.4) | collective-permute-done | bytes 589856 | tf_op jit(solution)/shard_map/ppermute | solution.py:283
  137.7 51.9 %shard_map.92 = f32[48,16,8,128]{3,2,1,0:T(8,128)} custom-call(f32[48,16,8,128]{3,2,1,0:T(8,128)} %shard_map.91.q_ref, f32[48,3,8,128]{3,2,1,0:T(8,128)S(1)} %collective-permute-done.4.low_ref, f32[48,3,8,128]{3,2,1,0:T(8,128)S(1)} %collective-permute-done.5.high_ref, f32[18,8,128]{2,1,0:T(8,128)S(1)} %pad_maximum_fusion.3.air_ref, ...), custom_call_target="tpu_custom_call" | custom-call | tf_op jit(solution)/shard_map/pallas_call | solution.py:251
  189.6 4.2 %copy.27 = f32[48,8,16,128]{3,2,1,0:T(8,128)} copy(f32[48,8,16,128]{3,1,2,0:T(8,128)} %bitcast.61) | data formatting | bytes 6291456 | tf_op jit(solution)/shard_map/transpose | solution.py:325
  (20 shorter events, 0.2 us)
Async XLA Ops:
  6.5 53.6 %all-reduce.2.cloned.1.call-start = ((), (), s32[]{:S(2)}) async-start(), calls=%async_computation | async-start | bytes 1048576 | tf_op jit(solution)/shard_map/psum | solution.py:312
  13.4 7.8 %copy-start.1 = (s32[512,2]{0,1:T(2,128)S(1)}, s32[512,2]{0,1:T(2,128)}, u32[]{:S(2)}) copy-start(s32[512,2]{0,1:T(2,128)} %param.14) | copy-start | bytes 12292
  13.4 7.8 %copy-start.2 = (f32[512]{0:T(512)S(1)}, f32[512]{0:T(512)}, u32[]{:S(2)}) copy-start(f32[512]{0:T(512)} %param.16) | copy-start | bytes 6148
  16.8 2.0 %copy-start = (f32[48,8,16,128]{3,1,2,0:T(8,128)}, f32[48,8,16,128]{3,1,2,0:T(8,128)S(1)}, u32[]{:S(2)}) copy-start(f32[48,8,16,128]{3,1,2,0:T(8,128)S(1)} %copy.33) | copy-start | bytes 9437188
  16.9 51.7 %collective-permute-start.1 = (f32[48,3,8,128]{3,2,1,0:T(8,128)S(1)}, f32[48,3,8,128]{3,2,1,0:T(8,128)S(1)}, u32[]{:S(2)}, u32[]{:S(2)}) collective-permute-start(f32[48,3,8,128]{3,2,1,0:T(8,128)S(1)} %get-tuple-element.7), channel_id=1, source_target_pairs={{1,0},{2,1},{3,2},{4,3},{5,4},{6,5},{7,6},{9,8},{10,9},{11,10},{12... | collective-permute-start | bytes 1769480 | tf_op jit(solution)/shard_map/ppermute | solution.py:284
  18.8 49.7 %collective-permute-start = (f32[48,3,8,128]{3,2,1,0:T(8,128)S(1)}, f32[48,3,8,128]{3,2,1,0:T(8,128)S(1)}, u32[]{:S(2)}, u32[]{:S(2)}) collective-permute-start(f32[48,3,8,128]{3,2,1,0:T(8,128)S(1)} %get-tuple-element.8), channel_id=1, source_target_pairs={{0,1},{1,2},{2,3},{3,4},{4,5},{5,6},{6,7},{8,9},{9,10},{10,11},{11... | collective-permute-start | bytes 1769480 | tf_op jit(solution)/shard_map/ppermute | solution.py:283
  60.9 7.6 %collective-permute-start.2 = (f32[2,2,3,8,128]{4,3,2,1,0:T(8,128)S(1)}, f32[2,2,3,8,128]{4,3,2,1,0:T(8,128)S(1)}, u32[]{:S(2)}, u32[]{:S(2)}) collective-permute-start(f32[2,2,3,8,128]{4,3,2,1,0:T(8,128)S(1)} %get-tuple-element.21), channel_id=1, source_target_pairs={{0,1},{1,2},{2,3},{3,4},{4,5},{5,6},{6,7},{8,9},{9,10},{10,11},{11... | collective-permute-start | bytes 147464 | tf_op jit(solution)/shard_map/ppermute | solution.py:283
  62.8 5.6 %collective-permute-start.3 = (f32[2,2,3,8,128]{4,3,2,1,0:T(8,128)S(1)}, f32[2,2,3,8,128]{4,3,2,1,0:T(8,128)S(1)}, u32[]{:S(2)}, u32[]{:S(2)}) collective-permute-start(f32[2,2,3,8,128]{4,3,2,1,0:T(8,128)S(1)} %get-tuple-element.22), channel_id=1, source_target_pairs={{1,0},{2,1},{3,2},{4,3},{5,4},{6,5},{7,6},{9,8},{10,9},{11,10},{12... | collective-permute-start | bytes 147464 | tf_op jit(solution)/shard_map/ppermute | solution.py:284
  124.6 9.3 %collective-permute-start.5 = (f32[48,3,8,128]{3,2,1,0:T(8,128)S(1)}, f32[48,3,8,128]{3,2,1,0:T(8,128)S(1)}, u32[]{:S(2)}, u32[]{:S(2)}) collective-permute-start(f32[48,3,8,128]{3,2,1,0:T(8,128)S(1)} %get-tuple-element.5), channel_id=1, source_target_pairs={{1,0},{2,1},{3,2},{4,3},{5,4},{6,5},{7,6},{9,8},{10,9},{11,10},{12... | collective-permute-start | bytes 1769480 | tf_op jit(solution)/shard_map/ppermute | solution.py:284
  126.5 11.2 %collective-permute-start.4 = (f32[48,3,8,128]{3,2,1,0:T(8,128)S(1)}, f32[48,3,8,128]{3,2,1,0:T(8,128)S(1)}, u32[]{:S(2)}, u32[]{:S(2)}) collective-permute-start(f32[48,3,8,128]{3,2,1,0:T(8,128)S(1)} %get-tuple-element.6), channel_id=1, source_target_pairs={{0,1},{1,2},{2,3},{3,4},{4,5},{5,6},{6,7},{8,9},{9,10},{10,11},{11... | collective-permute-start | bytes 1769480 | tf_op jit(solution)/shard_map/ppermute | solution.py:283
Sparse Core Ops, SparseCore 0:
  13.6 46.4 all-reduce.1
where the time goes:
time: 201 us
  Pallas kernels  107 us (53%)
  waiting for transfers between devices  45.9 us (23%)
  local copies, waits for them, and re-layouts  15.8 us (8%)
  between operations  14.9 us (7%)
  starting transfers between devices  14.2 us (7%)
  other arithmetic  3.25 us (2%)
    pallas_call x2, Pallas kernels, step(): pl.pallas_call(functools.partial(step_kernel, n, chunks), out_shape=jax.S...  107 us
    psum x1, waiting for transfers between devices, per_device(): weather = lax.psum(chosen, 'tracer')  37.2 us
    ppermute x3, starting transfers between devices, halos(): lax.ppermute(lax.slice_in_dim(block, 0, 3, axis=dim), 'tile', backward)  7.48 us
    ppermute x3, starting transfers between devices, halos(): lax.ppermute(lax.slice_in_dim(block, size - 3, size, axis=dim), 'tile', f...  6.72 us
    unnamed x10, local copies, waits for them, and re-layouts  5.93 us
    ppermute x3, waiting for transfers between devices, halos(): lax.ppermute(lax.slice_in_dim(block, 0, 3, axis=dim), 'tile', backward)  4.94 us
    transpose x1, local copies, waits for them, and re-layouts, per_device(): return jnp.swapaxes(mixing, 1, 2)  4.21 us
  transfers between devices with their start and end apart: 7, of which 3 were waited for; matrix products, arithmetic and copies ran while one was open for 4% of the time, Pallas kernels for 0%

commit v1 on v0

--- a/solution.py
+++ b/solution.py
@@ -49,10 +49,118 @@
     return pltpu.roll(faces, size - 1, axis) - faces
 
 
+def greet(peers, tile, tiles):
+    barrier = pltpu.get_barrier_semaphore()
+    for peer in peers[1:]:
+        pl.semaphore_signal(
+            barrier, inc=1, device_id={"tracer": peer}, device_id_type=pl.DeviceIdType.MESH
+        )
+    for side in range(2):
+
+        @pl.when(tile > 0 if side else tile < tiles - 1)
+        def _(side=side):
+            pl.semaphore_signal(
+                barrier,
+                inc=1,
+                device_id={"tile": tile - 1 if side else tile + 1},
+                device_id_type=pl.DeviceIdType.MESH,
+            )
+
+    sides = (tile > 0).astype(jnp.int32) + (tile < tiles - 1).astype(jnp.int32)
+    pl.semaphore_wait(barrier, len(peers) - 1 + sides)
+
+
+def weather_kernel(n, fields_ref, out_ref, side_send, side_recv, send_sem, recv_sem):
+    kinds, rows, levels, columns = fields_ref.shape
+    me = lax.axis_index("tracer")
+    peers = [lax.rem(me + k, n) for k in range(n)]
+    tile, tiles = lax.axis_index("tile"), lax.axis_size("tile")
+    greet(peers, tile, tiles)
+
+    def side_copy(side):
+        return pltpu.make_async_remote_copy(
+            src_ref=fields_ref.at[pl.ds(0, 2), 0 if side else rows - 1],
+            dst_ref=out_ref.at[me, pl.ds(0, 2), rows + 1 if side else 0],
+            send_sem=side_send.at[side],
+            recv_sem=side_recv.at[side],
+            device_id={"tile": tile - 1 if side else tile + 1},
+            device_id_type=pl.DeviceIdType.MESH,
+        )
+
+    for side in range(2):
+
+        @pl.when(tile > 0 if side else tile < tiles - 1)
+        def _(side=side):
+            side_copy(side).start()
+
+    blank = jnp.zeros((levels, columns), jnp.float32)
+    for kind in range(kinds):
+
+        @pl.loop(0, rows)
+        def _(r, kind=kind):
+            out_ref[me, kind, r + 1] = fields_ref[kind, r]
+
+    for kind in range(2, kinds):
+        out_ref[me, kind, 0] = blank
+        out_ref[me, kind, rows + 1] = blank
+    for side in range(2):
+
+        @pl.when(tile == tiles - 1 if side else tile == 0)
+        def _(side=side):
+            for kind in range(2):
+                out_ref[me, kind, rows + 1 if side else 0] = blank
+
+        @pl.when(tile < tiles - 1 if side else tile > 0)
+        def _(side=side):
+            side_copy(side).wait_recv()
+
+    def copy(k, source, target):
+        return pltpu.make_async_remote_copy(
+            src_ref=out_ref.at[source],
+            dst_ref=out_ref.at[source],
+            send_sem=send_sem.at[k - 1],
+            recv_sem=recv_sem.at[k - 1],
+            device_id={"tracer": target},
+            device_id_type=pl.DeviceIdType.MESH,
+        )
+
+    for k in range(1, n):
+        copy(k, me, peers[k]).start()
+    for k in range(1, n):
+        copy(k, peers[n - k], peers[n - k]).wait_recv()
+    for k in range(1, n):
+        copy(k, me, peers[k]).wait_send()
+    for side in range(2):
+
+        @pl.when(tile > 0 if side else tile < tiles - 1)
+        def _(side=side):
+            side_copy(side).wait_send()
+
+
+def all_weather(n, fields):
+    kinds, rows, levels, columns = fields.shape
+    vmem = pl.BlockSpec(memory_space=pltpu.VMEM)
+    return pl.pallas_call(
+        functools.partial(weather_kernel, n),
+        out_shape=jax.ShapeDtypeStruct((n, kinds, rows + 2, levels, columns), jnp.float32),
+        in_specs=[vmem],
+        out_specs=vmem,
+        scratch_shapes=[
+            pltpu.SemaphoreType.DMA((2,)),
+            pltpu.SemaphoreType.DMA((2,)),
+            pltpu.SemaphoreType.DMA((n - 1,)),
+            pltpu.SemaphoreType.DMA((n - 1,)),
+        ],
+        compiler_params=pltpu.CompilerParams(
+            collective_id=1, has_side_effects=True, vmem_limit_bytes=50 * 1024 * 1024
+        ),
+    )(fields)
+
+
 def step_kernel(
-    n, chunks, q_ref, low_ref, high_ref, air_ref, fx_ref, fy_ref, fz_ref, pick_ref, net_ref, rate_ref,
+    n, chunks, q_ref, air_ref, fx_ref, fy_ref, fz_ref, pick_ref, net_ref, rate_ref,
     out_ref, wx, wy, wz, inverse, lines, send_one, recv_one, send_two, recv_two, back,
-    send_sem, recv_sem, send_sem2, recv_sem2,
+    low_ref, high_ref, send_sem, recv_sem, send_sem2, recv_sem2, side_send, side_recv,
 ):
     tracers, rows, levels, columns = q_ref.shape
     padded = back.shape[0] // (rows * levels)
@@ -63,12 +171,34 @@
     me = lax.axis_index("tracer")
     peers = [lax.rem(me + k, n) for k in range(n)]
 
-    barrier = pltpu.get_barrier_semaphore()
-    for peer in peers[1:]:
-        pl.semaphore_signal(
-            barrier, inc=1, device_id={"tracer": peer}, device_id_type=pl.DeviceIdType.MESH
-        )
-    pl.semaphore_wait(barrier, n - 1)
+    tile, tiles = lax.axis_index("tile"), lax.axis_size("tile")
+    greet(peers, tile, tiles)
+
+    def side_copy(side, c):
+        span = pl.ds(c * in_chunk, in_chunk)
+        return pltpu.make_async_remote_copy(
+            src_ref=q_ref.at[span, pl.ds(0 if side else rows - 3, 3)],
+            dst_ref=(high_ref if side else low_ref).at[span],
+            send_sem=side_send.at[side, c],
+            recv_sem=side_recv.at[side, c],
+            device_id={"tile": tile - 1 if side else tile + 1},
+            device_id_type=pl.DeviceIdType.MESH,
+        )
+
+    for c in range(chunks):
+        for side in range(2):
+
+            @pl.when(tile > 0 if side else tile < tiles - 1)
+            def _(side=side, c=c):
+                side_copy(side, c).start()
+
+    @pl.when(tile == 0)
+    def _():
+        low_ref[...] = jnp.zeros_like(low_ref)
+
+    @pl.when(tile == tiles - 1)
+    def _():
+        high_ref[...] = jnp.zeros_like(high_ref)
 
     shape = (levels, columns)
     level = lax.broadcasted_iota(jnp.int32, shape, 0)
@@ -120,9 +250,14 @@
         )
 
     for c in range(chunks):
+        for side in range(2):
+
+            @pl.when(tile < tiles - 1 if side else tile > 0)
+            def _(side=side, c=c):
+                side_copy(side, c).wait_recv()
 
         @pl.loop(0, in_chunk)
-        def _(s):
+        def _(s, c=c):
             t = c * in_chunk + s
 
             def cell(r):
@@ -233,6 +368,13 @@
         for r in range(rows):
             out_ref[t, r] += back[pl.ds(r * levels * padded + t, levels, stride=padded), :]
 
+    for c in range(chunks):
+        for side in range(2):
+
+            @pl.when(tile > 0 if side else tile < tiles - 1)
+            def _(side=side, c=c):
+                side_copy(side, c).wait_send()
+
     for k in range(1, n):
         for c in range(chunks):
             copy_one(k, c).wait_send()
@@ -240,7 +382,7 @@
             copy_two(k, h).wait_send()
 
 
-def step(n, q, low, high, air, fx, fy, fz, pick, net, rate):
+def step(n, q, air, fx, fy, fz, pick, net, rate):
     tracers, rows, levels, columns = q.shape
     padded = net.shape[0] // n
     chunks = tracers // 16 if tracers % 16 == 0 else 1
@@ -251,7 +393,7 @@
     return pl.pallas_call(
         functools.partial(step_kernel, n, chunks),
         out_shape=jax.ShapeDtypeStruct(q.shape, f32),
-        in_specs=[vmem] * 10,
+        in_specs=[vmem] * 8,
         out_specs=vmem,
         scratch_shapes=[
             pltpu.VMEM((3, rows + 1, levels, columns), f32),
@@ -264,25 +406,19 @@
             pltpu.VMEM((n, held, padded, columns), bf16),
             pltpu.VMEM((n, held, padded, columns), bf16),
             pltpu.VMEM((rows * levels * padded, columns), f32),
+            pltpu.VMEM((tracers, 3, levels, columns), f32),
+            pltpu.VMEM((tracers, 3, levels, columns), f32),
             pltpu.SemaphoreType.DMA((n - 1, chunks)),
             pltpu.SemaphoreType.DMA((n - 1, chunks)),
             pltpu.SemaphoreType.DMA((n - 1, PIECES)),
             pltpu.SemaphoreType.DMA((n - 1, PIECES)),
+            pltpu.SemaphoreType.DMA((2, chunks)),
+            pltpu.SemaphoreType.DMA((2, chunks)),
         ],
         compiler_params=pltpu.CompilerParams(
             collective_id=0, has_side_effects=True, vmem_limit_bytes=50 * 1024 * 1024
         ),
-    )(q, low, high, air, fx, fy, fz, pick, net, rate)
-
-
-def halos(block, dim):
-    count = lax.axis_size("tile")
-    forward = [(i, i + 1) for i in range(count - 1)]
-    backward = [(target, source) for source, target in forward]
-    size = block.shape[dim]
-    low = lax.ppermute(lax.slice_in_dim(block, size - 3, size, axis=dim), "tile", forward)
-    high = lax.ppermute(lax.slice_in_dim(block, 0, 3, axis=dim), "tile", backward)
-    return low, high
+    )(q, air, fx, fy, fz, pick, net, rate)
 
 
 def pad_blocks(matrix, n, padded):
@@ -307,21 +443,17 @@
     mixing = jnp.swapaxes(tracers, 1, 2)
     rows = mixing.shape[1]
     fields = jnp.swapaxes(jnp.concatenate([air_mass, flux_x, flux_y, flux_z], 0), 1, 2)
-    mine = lax.axis_index("tracer")
-    chosen = jnp.stack([jnp.where(record_of_step[s] == mine, fields, 0.0) for s in range(STEPS)])
-    weather = lax.psum(chosen, "tracer")
-    below, above = halos(weather[:, :2], 2)
-    place = lax.axis_index("tile") * rows + lax.broadcasted_iota(jnp.int32, weather.shape[2:], 0)
-    level = lax.broadcasted_iota(jnp.int32, weather.shape[2:], 1)
-    column = lax.broadcasted_iota(jnp.int32, weather.shape[2:], 2)
+    gathered = all_weather(n, fields)
+    place = lax.axis_index("tile") * rows + lax.broadcasted_iota(jnp.int32, (rows + 1, 1, 1), 0)
+    level = lax.broadcasted_iota(jnp.int32, fields.shape[1:], 1)
+    column = lax.broadcasted_iota(jnp.int32, fields.shape[1:], 2)
     for s in range(STEPS):
-        air, east, south, bottom = (weather[s, i] for i in range(4))
-        air = jnp.concatenate([below[s, 0, 2:3], air, above[s, 0, :1]], 0)
-        east = jnp.concatenate([jnp.where(place == 0, 0.0, east), above[s, 1, :1]], 0)
-        south = jnp.where(column == 0, 0.0, south)
-        bottom = jnp.where(level == 0, 0.0, bottom)
-        low, high = halos(mixing, 1)
-        mixing = step(n, mixing, low, high, air, east, south, bottom, pick, net, rate)
+        weather = lax.dynamic_index_in_dim(gathered, record_of_step[s], 0, keepdims=False)
+        air = weather[0]
+        east = jnp.where(place == 0, 0.0, weather[1, 1:])
+        south = jnp.where(column == 0, 0.0, weather[2, 1 : rows + 1])
+        bottom = jnp.where(level == 0, 0.0, weather[3, 1 : rows + 1])
+        mixing = step(n, mixing, air, east, south, bottom, pick, net, rate)
     return jnp.swapaxes(mixing, 1, 2)
 
 

time: 201 us -> 152 us (0.76)
  waiting for transfers between devices: 45.9 us -> 0 us
  Pallas kernels: 107 us -> 132 us
  starting transfers between devices: 14.2 us -> 0 us
  between operations: 14.9 us -> 3.75 us
    psum x1 -> x0, waiting for transfers between devices: 37.2 us -> none  [per_device(): weather = lax.psum(chosen, 'tracer')]
    pallas_call x0 -> x1, Pallas kernels: none -> 18.3 us  [all_weather(): pl.pallas_call(functools.partial(weather_kernel, n), out_shape=jax.ShapeD...]
    ppermute x6 -> x0, starting transfers between devices: 14.2 us -> none  [the longest x3 7.48 us: halos(): lax.ppermute(lax.slice_in_dim(block, 0, 3, axis=dim), 'tile', backward)]
    ppermute x6 -> x0, waiting for transfers between devices: 8.77 us -> none  [the longest x3 4.94 us: halos(): lax.ppermute(lax.slice_in_dim(block, 0, 3, axis=dim), 'tile', backward)]
    pallas_call x2, Pallas kernels: 107 us -> 113 us  [step(): pl.pallas_call(functools.partial(step_kernel, n, chunks), out_shape=jax.S...]
    slice x4 -> x1, local copies, waits for them, and re-layouts: 3.57 us -> 1.31 us  [per_device(): record_of_step[s]]
    unnamed x10 -> x7, local copies, waits for them, and re-layouts: 5.93 us -> 6.54 us
  transfers between devices with their start and end apart: 7 -> 0, of which waited for: 3 -> 0; matrix products, arithmetic and copies ran while one was open for 4% -> 0% of each run, Pallas kernels for 0% -> 0%
where the time goes in v1:
time: 152 us; the launch traced here: 151 us
  Pallas kernels  132 us (87%)
  local copies, waits for them, and re-layouts  13.9 us (9%)
  between operations  3.75 us (2%)
    pallas_call x2, Pallas kernels, step(): pl.pallas_call(functools.partial(step_kernel, n, chunks), out_shape=jax.S...  113 us
    pallas_call x1, Pallas kernels, all_weather(): pl.pallas_call(functools.partial(weather_kernel, n), out_shape=jax.ShapeD...  18.3 us
    unnamed x7, local copies, waits for them, and re-layouts  6.54 us
    transpose x1, local copies, waits for them, and re-layouts, per_device(): return jnp.swapaxes(mixing, 1, 2)  4.21 us

profile of v1, /device:TPU:8, one launch (start us, length us, event | category | flops | bytes accessed | tf_op | source)
XLA Modules:
  0.0 150.7 jit_solution(7311999309588996190)
XLA Ops:
  0.0 1.3 fusion.9
  5.0 0.8 fusion.8
  5.7 0.9 copy.19
  6.6 0.9 copy.20
  7.5 0.9 copy.21
  8.3 0.9 copy.22
  9.2 1.1 fusion.1.net_ref
  10.3 0.8 copy.24.rate_ref
  11.2 0.1 convert_convert_fusion
  11.3 0.2 copy.23.pick_ref
  11.5 0.0 copy-start
  11.5 18.3 %shard_map.91 = f32[4,4,18,8,128]{4,3,2,1,0:T(8,128)S(1)} custom-call(f32[4,16,8,128]{3,2,1,0:T(8,128)S(1)} %maximum_bitcast_fusion.fields_ref), custom_call_target="tpu_custom_call" | custom-call | tf_op jit(solution)/shard_map/pallas_call | solution.py:143
  29.9 0.1 fusion.2
  30.0 0.1 fusion.6
  30.1 0.0 copy-done
  30.1 3.1 %copy.29 = f32[48,8,16,128]{3,1,2,0:T(8,128)} copy(f32[48,8,16,128]{3,2,1,0:T(8,128)S(1)} %copy-done) | data formatting | bytes 6291456 | tf_op args[0]
  33.2 57.6 %shard_map.92.q_ref = f32[48,16,8,128]{3,2,1,0:T(8,128)} custom-call(f32[48,16,8,128]{3,2,1,0:T(8,128)} %bitcast.46, f32[18,8,128]{2,1,0:T(8,128)S(1)} %get-tuple-element.8.air_ref, f32[17,8,128]{2,1,0:T(8,128)S(1)} %get-tuple-element.18.fx_ref, f32[16,8,128]{2,1,0:T(8,128)S(1)} %get-tuple-element.12.fy_ref, f32[16,8,128]{2,1,0:T(8,128)S(1)} %get-tuple-element.11.fz_ref, ...), custom_call_target="tpu_custom_call" | custom-call | tf_op jit(solution)/shard_map/pallas_call | solution.py:393
  90.7 55.7 %shard_map.93 = f32[48,16,8,128]{3,2,1,0:T(8,128)} custom-call(f32[48,16,8,128]{3,2,1,0:T(8,128)} %shard_map.92.q_ref, f32[18,8,128]{2,1,0:T(8,128)S(1)} %get-tuple-element.7.air_ref, f32[17,8,128]{2,1,0:T(8,128)S(1)} %get-tuple-element.17.fx_ref, f32[16,8,128]{2,1,0:T(8,128)S(1)} %get-tuple-element.15.fy_ref, f32[16,8,128]{2,1,0:T(8,128)S(1)} %get-tuple-element.16.fz_ref, ...), custom_call_target="tpu_custom_call" | custom-call | tf_op jit(solution)/shard_map/pallas_call | solution.py:393
  146.5 4.2 %copy.27 = f32[48,8,16,128]{3,2,1,0:T(8,128)} copy(f32[48,8,16,128]{3,1,2,0:T(8,128)} %bitcast.45) | data formatting | bytes 6291456 | tf_op jit(solution)/shard_map/transpose | solution.py:457
  (7 shorter events, 0.1 us)
Async XLA Ops:
  11.5 18.5 %copy-start = (f32[48,8,16,128]{3,2,1,0:T(8,128)S(1)}, f32[48,8,16,128]{3,2,1,0:T(8,128)}, u32[]{:S(2)}) copy-start(f32[48,8,16,128]{3,2,1,0:T(8,128)} %param.9) | copy-start | bytes 9437188
